TPU v7x, 32 devices: a whole 2x2x4 slice. The times are simulated.
32 devices in a mesh: row: 4 (over x, core), col: 8 (over z, y).
Axes of the slice: x: 2, y: 2, z: 4, core: 2. Of those that a mesh axis runs over, the one named last changes fastest.
Arguments:
- gradient: bfloat16 [5120, 5120], P('row', 'col'), may hold values from -6 to 6
- left_basis: bfloat16 [5120, 5120], P('row', 'col'), may hold values from -0.078125 to 0.078125
- right_basis: bfloat16 [5120, 5120], P('row', 'col'), may hold values from -0.078125 to 0.078125
- first_moment: float32 [5120, 5120], P('row', 'col'), may hold values from -4 to 4
- second_moment: float32 [5120, 5120], P('row', 'col'), may hold values from 0.05 to 2
Outputs:
- update: bfloat16 [5120, 5120], P('row', 'col')
- new_first: float32 [5120, 5120], P('row', 'col')
- new_second: float32 [5120, 5120], P('row', 'col')
All inputs are finite; a program needn't handle non-finite values.
Results may differ from a plain program's by a relative error of at most 0.006.
Values may be sent and summed in bfloat16 or wider, within the bound.
A program may use at most 192 MiB of HBM per device.

v0:
```python
import jax
import jax.numpy as jnp
from jax import lax
from jax.sharding import PartitionSpec as P

STEP = 10


def body(gradient, left_basis, right_basis, first_moment, second_moment):
    left_panel = lax.all_gather(left_basis, "col", axis=1, tiled=True)
    right_panel = lax.all_gather(right_basis, "row", axis=0, tiled=True)
    columns = left_panel
    left_rotated = lax.psum_scatter(
        lax.dot_general(
            columns, gradient, (((0,), (0,)), ((), ())), preferred_element_type=jnp.float32
        ),
        "row",
        scatter_dimension=0,
        tiled=True,
    ).astype(jnp.bfloat16)
    rotated = jnp.dot(
        lax.all_gather(left_rotated, "col", axis=1, tiled=True),
        right_panel,
        preferred_element_type=jnp.float32,
    )
    new_first = 0.9 * first_moment + 0.1 * rotated
    new_second = 0.95 * second_moment + 0.05 * rotated * rotated
    first_fix = 1.0 - 0.9**STEP
    second_fix = 1.0 - 0.95**STEP
    direction = (new_first / first_fix / (jnp.sqrt(new_second / second_fix) + 1e-08)).astype(
        jnp.bfloat16
    )
    columns = left_panel
    back_left = jnp.dot(
        columns,
        lax.all_gather(direction, "row", axis=0, tiled=True),
        preferred_element_type=jnp.float32,
    ).astype(jnp.bfloat16)
    partial_terms = lax.dot_general(
        back_left, right_panel, (((1,), (1,)), ((), ())), preferred_element_type=jnp.float32
    )
    update = lax.psum_scatter(partial_terms, "col", scatter_dimension=1, tiled=True)
    return (update.astype(jnp.bfloat16), new_first, new_second)


def solution(mesh):
    placed = (P("row", "col"), P("row", "col"), P("row", "col"), P("row", "col"), P("row", "col"))
    return jax.shard_map(
        body,
        mesh=mesh,
        in_specs=placed,
        out_specs=(P("row", "col"), P("row", "col"), P("row", "col")),
        check_vma=False,
    )
```

profile of v0, /device:TPU:8, one launch (start us, length us, event | category | flops | bytes accessed | tf_op | source)
XLA Modules:
  0.0 1084.3 jit_solution(7324474922350682983)
XLA Ops:
  7.2 0.0 copy-start
  7.2 0.0 all-gather.5.cloned.1.call-start
  7.2 0.7 all-gather.5.cloned.1.call-update
  7.9 0.0 reduce-scatter.3.cloned.1.call-start
  8.0 184.5 %all-gather.5.cloned.1.call-done = bf16[1280,5120]{1,0:T(8,128)(2,1)} async-done(((bf16[1280,640]{1,0:T(8,128)(2,1)}), bf16[1280,5120]{1,0:T(8,128)(2,1)}) %all-gather.5.cloned.1.call-update) | async-done | bytes 13107216 | tf_op jit(solution)/shard_map/all_gather | solution.py:10
  192.4 0.0 copy-done
  192.4 16.3 %fusion.3 = f32[5120,640]{1,0:T(8,128)} fusion(bf16[1280,5120]{1,0:T(8,128)(2,1)} %all-gather.5.cloned.1.call-done, bf16[1280,640]{1,0:T(8,128)(2,1)S(1)} %copy-done), kind=kOutput, calls=%fused_computation.6 | convolution fusion | flops 8388608000 | bytes 27852800 | tf_op jit(solution)/shard_map/dot_general | solution.py:14
  208.7 0.0 reduce-scatter.3.cloned.1.call-update
  208.7 0.0 all-gather.9.cloned.1.call-start
  208.8 0.7 all-gather.9.cloned.1.call-update
  209.5 0.0 all-gather.7.cloned.1.call-start
  209.5 101.9 %reduce-scatter.3.cloned.1.call-done = f32[1280,640]{1,0:T(8,128)} async-done(((f32[5120,640]{1,0:T(8,128)}), f32[1280,640]{1,0:T(8,128)}) %reduce-scatter.3.cloned.1.call-update) | async-done | bytes 3276816 | tf_op jit(solution)/shard_map/reduce_scatter | solution.py:13
  311.4 3.3 convert_element_type.13
  314.7 0.0 all-gather.7.cloned.1.call-update
  314.7 0.0 all-gather.11.cloned.1.call-start
  314.7 46.1 %all-gather.9.cloned.1.call-done = bf16[5120,640]{1,0:T(8,128)(2,1)} async-done(((bf16[1280,640]{1,0:T(8,128)(2,1)}), bf16[5120,640]{1,0:T(8,128)(2,1)}) %all-gather.9.cloned.1.call-update) | async-done | bytes 6553616 | tf_op jit(solution)/shard_map/all_gather | solution.py:11
  360.9 183.7 %all-gather.7.cloned.1.call-done = bf16[1280,5120]{1,0:T(8,128)(2,1)} async-done(((bf16[1280,640]{1,0:T(8,128)(2,1)}), bf16[1280,5120]{1,0:T(8,128)(2,1)}) %all-gather.7.cloned.1.call-update) | async-done | bytes 13107216 | tf_op jit(solution)/shard_map/all_gather | solution.py:22
  544.6 20.2 %divide_convert_fusion = (bf16[1280,640]{1,0:T(8,128)(2,1)}, f32[1280,640]{1,0:T(8,128)}, f32[1280,640]{1,0:T(8,128)}) fusion(f32[1280,640]{1,0:T(8,128)} %param.8, f32[1280,640]{1,0:T(8,128)} %param.9, bf16[1280,5120]{1,0:T(8,128)(2,1)} %all-gather.7.cloned.1.call-done, bf16[5120,640]{1,0:T(8,128)(2,1)} %all-gather.9.cloned.1.call-done), kind=kOutput, calls=%fused_computation.2 | convolution fusion | flops 8398438400 | bytes 34406400 | tf_op jit(solution)/shard_map/dot_general | solution.py:21
  564.8 0.0 all-gather.11.cloned.1.call-update
  564.8 0.2 reduce-scatter.5.cloned.1.call-start
  565.0 47.8 %all-gather.11.cloned.1.call-done = bf16[5120,640]{1,0:T(8,128)(2,1)} async-done(((bf16[1280,640]{1,0:T(8,128)(2,1)}), bf16[5120,640]{1,0:T(8,128)(2,1)}) %all-gather.11.cloned.1.call-update) | async-done | bytes 6553616 | tf_op jit(solution)/shard_map/all_gather | solution.py:36
  612.8 44.0 %fusion.1 = f32[1280,5120]{1,0:T(8,128)} fusion(bf16[5120,640]{1,0:T(8,128)(2,1)} %all-gather.9.cloned.1.call-done, bf16[5120,640]{1,0:T(8,128)(2,1)} %all-gather.11.cloned.1.call-done, bf16[1280,5120]{1,0:T(8,128)(2,1)} %all-gather.5.cloned.1.call-done), kind=kOutput, calls=%fused_computation.5 | convolution fusion | flops 16778035200 | bytes 52428800 | tf_op jit(solution)/shard_map/dot_general | solution.py:39
  656.8 0.0 reduce-scatter.5.cloned.1.call-update
  656.8 0.0 copy-start.1
  656.9 417.4 %reduce-scatter.5.cloned.1.call-done = f32[1280,640]{1,0:T(8,128)} async-done(((f32[1280,5120]{1,0:T(8,128)}), f32[1280,640]{1,0:T(8,128)}) %reduce-scatter.5.cloned.1.call-update) | async-done | bytes 3276816 | tf_op jit(solution)/shard_map/reduce_scatter | solution.py:42
  1074.2 3.3 convert_element_type.16
  1077.5 0.0 copy-done.1
Async XLA Ops:
  7.2 185.3 %copy-start = (bf16[1280,640]{1,0:T(8,128)(2,1)S(1)}, bf16[1280,640]{1,0:T(8,128)(2,1)}, u32[]{:S(2)}) copy-start(bf16[1280,640]{1,0:T(8,128)(2,1)} %param.5) | copy-start | bytes 4915204
  7.2 185.3 %all-gather.5.cloned.1.call-start = ((), (), s32[]{:S(2)}) async-start(), calls=%async_computation.2 | async-start | bytes 14745600 | tf_op jit(solution)/shard_map/all_gather | solution.py:10
  7.9 303.5 %reduce-scatter.3.cloned.1.call-start = ((), (), s32[]{:S(2)}) async-start(), calls=%async_computation.3 | async-start | bytes 16384000 | tf_op jit(solution)/shard_map/reduce_scatter | solution.py:13
  208.7 152.1 %all-gather.9.cloned.1.call-start = ((), (), s32[]{:S(2)}) async-start(), calls=%async_computation.5 | async-start | bytes 8192000 | tf_op jit(solution)/shard_map/all_gather | solution.py:11
  209.5 335.1 %all-gather.7.cloned.1.call-start = ((), (), s32[]{:S(2)}) async-start(), calls=%async_computation.4 | async-start | bytes 14745600 | tf_op jit(solution)/shard_map/all_gather | solution.py:22
  314.7 298.2 %all-gather.11.cloned.1.call-start = ((), (), s32[]{:S(2)}) async-start(), calls=%async_computation.6 | async-start | bytes 8192000 | tf_op jit(solution)/shard_map/all_gather | solution.py:36
  564.8 509.4 %reduce-scatter.5.cloned.1.call-start = ((), (), s32[]{:S(2)}) async-start(), calls=%async_computation.7 | async-start | bytes 29491200 | tf_op jit(solution)/shard_map/reduce_scatter | solution.py:42
  656.8 420.6 %copy-start.1 = (bf16[1280,640]{1,0:T(8,128)(2,1)S(1)}, bf16[1280,640]{1,0:T(8,128)(2,1)}, u32[]{:S(2)}) copy-start(bf16[1280,640]{1,0:T(8,128)(2,1)} %param.5) | copy-start | bytes 4915204
Sparse Core Ops, SparseCore 0:
  10.2 182.1 all-gather.4
  208.8 102.5 reduce-scatter.2
  313.0 47.8 all-gather.8
  363.5 180.9 all-gather.6
  564.9 47.8 all-gather.10
  657.0 417.2 reduce-scatter.4
where the time goes:
time: 1090 us; the launch traced here: 1080 us
  waiting for transfers between devices  983 us (90%)
  matrix products  80.4 us (7%)
  between operations  14.1 us (1%)
    reduce_scatter x1, waiting for transfers between devices, body(): lax.psum_scatter(partial_terms, 'col', scatter_dimension=1, tiled=True)  417 us
    all_gather x1, waiting for transfers between devices, body(): left_panel = lax.all_gather(left_basis, 'col', axis=1, tiled=True)  184 us
    all_gather x1, waiting for transfers between devices, body(): lax.all_gather(left_rotated, 'col', axis=1, tiled=True)  184 us
    reduce_scatter x1, waiting for transfers between devices, body(): lax.psum_scatter(lax.dot_general(columns, gradient, (((0,), (0,)), ((), (...  102 us
    all_gather x1, waiting for transfers between devices, body(): lax.all_gather(direction, 'row', axis=0, tiled=True)  47.8 us
    all_gather x1, waiting for transfers between devices, body(): right_panel = lax.all_gather(right_basis, 'row', axis=0, tiled=True)  46.1 us
    dot_general x1, matrix products, body(): lax.dot_general(back_left, right_panel, (((1,), (1,)), ((), ())), preferr...  44 us
  transfers between devices with their start and end apart: 6, of which 6 were waited for; matrix products, arithmetic and copies ran while one was open for 0% of the time, Pallas kernels for 0%

commit v1 on v0

--- a/solution.py
+++ b/solution.py
@@ -13,7 +13,7 @@
     left_rotated = lax.psum_scatter(
         lax.dot_general(
             columns, gradient, (((0,), (0,)), ((), ())), preferred_element_type=jnp.float32
-        ),
+        ).astype(jnp.bfloat16),
         "row",
         scatter_dimension=0,
         tiled=True,
@@ -39,7 +39,7 @@
     partial_terms = lax.dot_general(
         back_left, right_panel, (((1,), (1,)), ((), ())), preferred_element_type=jnp.float32
     )
-    update = lax.psum_scatter(partial_terms, "col", scatter_dimension=1, tiled=True)
+    update = lax.psum_scatter(partial_terms.astype(jnp.bfloat16), "col", scatter_dimension=1, tiled=True)
     return (update.astype(jnp.bfloat16), new_first, new_second)
 
 

time: 1090 us -> 857 us (0.79)
  waiting for transfers between devices: 983 us -> 739 us
  local copies, waits for them, and re-layouts: 0.02 us -> 21.2 us
    reduce_scatter x1 -> x0, waiting for transfers between devices: 417 us -> none  [body(): lax.psum_scatter(partial_terms, 'col', scatter_dimension=1, tiled=True)]
    unnamed x6 -> x7, waiting for transfers between devices: 1.43 us -> 214 us
    reduce_scatter x1, waiting for transfers between devices: 102 us -> 59.5 us  [body(): lax.psum_scatter(lax.dot_general(columns, gradient, (((0,), (0,)), ((), (...]
    unnamed x4 -> x6, local copies, waits for them, and re-layouts: 0.02 us -> 21.2 us
where the time goes in v1:
time: 857 us; the launch traced here: 853 us
  waiting for transfers between devices  739 us (86%)
  matrix products  78.6 us (9%)
  local copies, waits for them, and re-layouts  21.2 us (2%)
  between operations  14.1 us (2%)
    unnamed x7, waiting for transfers between devices  214 us
    all_gather x1, waiting for transfers between devices, body(): left_panel = lax.all_gather(left_basis, 'col', axis=1, tiled=True)  184 us
    all_gather x1, waiting for transfers between devices, body(): lax.all_gather(left_rotated, 'col', axis=1, tiled=True)  183 us
    reduce_scatter x1, waiting for transfers between devices, body(): lax.psum_scatter(lax.dot_general(columns, gradient, (((0,), (0,)), ((), (...  59.5 us
    all_gather x1, waiting for transfers between devices, body(): right_panel = lax.all_gather(right_basis, 'row', axis=0, tiled=True)  49.5 us
    all_gather x1, waiting for transfers between devices, body(): lax.all_gather(direction, 'row', axis=0, tiled=True)  47.8 us
    dot_general x1, matrix products, body(): lax.dot_general(back_left, right_panel, (((1,), (1,)), ((), ())), preferr...  43.2 us
    unnamed x6, local copies, waits for them, and re-layouts  21.2 us
  transfers between devices with their start and end apart: 6, of which 6 were waited for; matrix products, arithmetic and copies ran while one was open for 0% of the time, Pallas kernels for 0%

profile of v1, /device:TPU:8, one launch (start us, length us, event | category | flops | bytes accessed | tf_op | source)
XLA Modules:
  0.0 853.3 jit_solution(17402575347198834284)
XLA Ops:
  7.2 0.0 copy-start
  7.2 0.0 all-gather.5.cloned.1.call-start
  7.2 0.7 all-gather.5.cloned.1.call-update
  7.9 0.0 reduce-scatter.5.cloned.1.call-start
  8.0 184.5 %all-gather.5.cloned.1.call-done = bf16[1280,5120]{1,0:T(8,128)(2,1)} async-done(((bf16[1280,640]{1,0:T(8,128)(2,1)}), bf16[1280,5120]{1,0:T(8,128)(2,1)}) %all-gather.5.cloned.1.call-update) | async-done | bytes 13107216 | tf_op jit(solution)/shard_map/all_gather | solution.py:10
  192.4 0.0 copy-done
  192.4 15.2 %convolution_convert_fusion.1 = bf16[5120,640]{1,0:T(8,128)(2,1)} fusion(bf16[1280,5120]{1,0:T(8,128)(2,1)} %all-gather.5.cloned.1.call-done, bf16[1280,640]{1,0:T(8,128)(2,1)S(1)} %copy-done), kind=kOutput, calls=%fused_computation.1 | convolution fusion | flops 8391884800 | bytes 21299200 | tf_op jit(solution)/shard_map/dot_general | solution.py:14
  207.7 0.0 reduce-scatter.5.cloned.1.call-update
  207.7 0.0 all-gather.9.cloned.1.call-start
  207.7 0.7 all-gather.9.cloned.1.call-update
  208.4 0.0 all-gather.7.cloned.1.call-start
  208.5 59.5 %reduce-scatter.5.cloned.1.call-done = bf16[1280,640]{1,0:T(8,128)(2,1)} async-done(((bf16[5120,640]{1,0:T(8,128)(2,1)}), bf16[1280,640]{1,0:T(8,128)(2,1)}) %reduce-scatter.5.cloned.1.call-update) | async-done | bytes 1638416 | tf_op jit(solution)/shard_map/reduce_scatter | solution.py:13
  268.0 0.0 all-gather.7.cloned.1.call-update
  268.0 0.0 all-gather.11.cloned.1.call-start
  268.0 49.5 %all-gather.9.cloned.1.call-done = bf16[5120,640]{1,0:T(8,128)(2,1)} async-done(((bf16[1280,640]{1,0:T(8,128)(2,1)}), bf16[5120,640]{1,0:T(8,128)(2,1)}) %all-gather.9.cloned.1.call-update) | async-done | bytes 6553616 | tf_op jit(solution)/shard_map/all_gather | solution.py:11
  317.5 183.4 %all-gather.7.cloned.1.call-done = bf16[1280,5120]{1,0:T(8,128)(2,1)} async-done(((bf16[1280,640]{1,0:T(8,128)(2,1)}), bf16[1280,5120]{1,0:T(8,128)(2,1)}) %all-gather.7.cloned.1.call-update) | async-done | bytes 13107216 | tf_op jit(solution)/shard_map/all_gather | solution.py:22
  500.9 20.2 %divide_convert_fusion = (bf16[1280,640]{1,0:T(8,128)(2,1)}, f32[1280,640]{1,0:T(8,128)}, f32[1280,640]{1,0:T(8,128)}) fusion(f32[1280,640]{1,0:T(8,128)} %param.8, f32[1280,640]{1,0:T(8,128)} %param.9, bf16[1280,5120]{1,0:T(8,128)(2,1)} %all-gather.7.cloned.1.call-done, bf16[5120,640]{1,0:T(8,128)(2,1)} %all-gather.9.cloned.1.call-done), kind=kOutput, calls=%fused_computation.4 | convolution fusion | flops 8398438400 | bytes 34406400 | tf_op jit(solution)/shard_map/dot_general | solution.py:21
  521.1 0.0 all-gather.11.cloned.1.call-update
  521.1 0.2 reduce-scatter.7.cloned.1.call-start
  521.4 47.8 %all-gather.11.cloned.1.call-done = bf16[5120,640]{1,0:T(8,128)(2,1)} async-done(((bf16[1280,640]{1,0:T(8,128)(2,1)}), bf16[5120,640]{1,0:T(8,128)(2,1)}) %all-gather.11.cloned.1.call-update) | async-done | bytes 6553616 | tf_op jit(solution)/shard_map/all_gather | solution.py:36
  569.2 43.2 %convolution_convert_fusion = bf16[1280,5120]{1,0:T(8,128)(2,1)} fusion(bf16[5120,640]{1,0:T(8,128)(2,1)} %all-gather.9.cloned.1.call-done, bf16[5120,640]{1,0:T(8,128)(2,1)} %all-gather.11.cloned.1.call-done, bf16[1280,5120]{1,0:T(8,128)(2,1)} %all-gather.5.cloned.1.call-done), kind=kOutput, calls=%fused_computation | convolution fusion | flops 16784588800 | bytes 39321600 | tf_op jit(solution)/shard_map/dot_general | solution.py:39
  612.4 17.6 %copy.8 = bf16[1280,5120]{0,1:T(8,128)(2,1)} copy(bf16[1280,5120]{1,0:T(8,128)(2,1)} %convolution_convert_fusion) | data formatting | bytes 26214400
  630.0 0.0 reduce-scatter.7.cloned.1.call-update
  630.0 0.0 copy-start.1
  630.0 212.8 %reduce-scatter.7.cloned.1.call-done = bf16[640,1280]{1,0:T(8,128)(2,1)} async-done(((bf16[5120,1280]{1,0:T(8,128)(2,1)}), bf16[640,1280]{1,0:T(8,128)(2,1)}) %reduce-scatter.7.cloned.1.call-update) | async-done | bytes 1638416
  842.9 3.5 copy.9
  846.4 0.0 copy-done.1
Async XLA Ops:
  7.2 185.3 %copy-start = (bf16[1280,640]{1,0:T(8,128)(2,1)S(1)}, bf16[1280,640]{1,0:T(8,128)(2,1)}, u32[]{:S(2)}) copy-start(bf16[1280,640]{1,0:T(8,128)(2,1)} %param.5) | copy-start | bytes 4915204
  7.2 185.3 %all-gather.5.cloned.1.call-start = ((), (), s32[]{:S(2)}) async-start(), calls=%async_computation.2 | async-start | bytes 14745600 | tf_op jit(solution)/shard_map/all_gather | solution.py:10
  7.9 260.1 %reduce-scatter.5.cloned.1.call-start = ((), (), s32[]{:S(2)}) async-start(), calls=%async_computation.3 | async-start | bytes 8192000 | tf_op jit(solution)/shard_map/reduce_scatter | solution.py:13
  207.7 109.8 %all-gather.9.cloned.1.call-start = ((), (), s32[]{:S(2)}) async-start(), calls=%async_computation.5 | async-start | bytes 8192000 | tf_op jit(solution)/shard_map/all_gather | solution.py:11
  208.4 292.5 %all-gather.7.cloned.1.call-start = ((), (), s32[]{:S(2)}) async-start(), calls=%async_computation.4 | async-start | bytes 14745600 | tf_op jit(solution)/shard_map/all_gather | solution.py:22
  268.0 301.2 %all-gather.11.cloned.1.call-start = ((), (), s32[]{:S(2)}) async-start(), calls=%async_computation.6 | async-start | bytes 8192000 | tf_op jit(solution)/shard_map/all_gather | solution.py:36
  521.1 321.8 %reduce-scatter.7.cloned.1.call-start = ((), (), s32[]{:S(2)}) async-start(), calls=%async_computation.7 | async-start | bytes 14745600
  630.0 216.4 %copy-start.1 = (bf16[1280,640]{1,0:T(8,128)(2,1)S(1)}, bf16[1280,640]{1,0:T(8,128)(2,1)}, u32[]{:S(2)}) copy-start(bf16[1280,640]{1,0:T(8,128)(2,1)} %param.5) | copy-start | bytes 4915204
Sparse Core Ops, SparseCore 0:
  10.2 182.1 all-gather.4
  207.8 60.1 reduce-scatter.4
  269.6 47.8 all-gather.8
  319.9 180.9 all-gather.6
  521.2 47.8 all-gather.10
  630.2 212.6 reduce-scatter.6

commit v2 on v0

v2 whole, which is shorter than its diff:
```python
import functools
import jax
import jax.numpy as jnp
from jax import lax
from jax.experimental import pallas as pl
from jax.experimental.pallas import tpu as pltpu
from jax.sharding import PartitionSpec as P

STEP = 10
LINE = 4
MESH = pl.DeviceIdType.MESH
BF16 = jnp.bfloat16
F32 = jnp.float32


def tile_of(size, wanted):
    return wanted if size % wanted == 0 else size


class Place:
    def __init__(self, rows, cols):
        self.rows, self.cols = rows, cols
        self.breadth = cols // LINE
        self.r, self.c = lax.axis_index("row"), lax.axis_index("col")
        self.a, self.b = self.c // self.breadth, self.c % self.breadth

    def beside(self, k):
        return (self.b + k) % self.breadth

    def row_peer(self, k):
        return (self.r + k) % self.rows

    def greet(self, across, along):
        barrier = pltpu.get_barrier_semaphore()

        def hello(row, col):
            pl.semaphore_signal(barrier, inc=1, device_id=(row, col), device_id_type=MESH)

        count = 0
        if along:
            for k in range(1, self.breadth):
                hello(self.r, self.a * self.breadth + self.beside(k))
                count += 1

            @pl.when(self.a > 0)
            def _():
                hello(self.r, self.c - self.breadth)

            @pl.when(self.a < LINE - 1)
            def _():
                hello(self.r, self.c + self.breadth)

        if across:
            for k in range(1, self.rows):
                hello(self.row_peer(k), self.c)
                count += 1
        if not along:
            pl.semaphore_wait(barrier, count)
            return
        end = (self.a == 0) | (self.a == LINE - 1)

        @pl.when(end)
        def _():
            pl.semaphore_wait(barrier, count + 1)

        @pl.when(jnp.logical_not(end))
        def _():
            pl.semaphore_wait(barrier, count + 2)


def remote(src, dst, send, recv, row, col):
    return pltpu.make_async_remote_copy(
        src_ref=src,
        dst_ref=dst,
        send_sem=send,
        recv_sem=recv,
        device_id=(row, col),
        device_id_type=MESH,
    )


def gather_along(at, panel, send, recv, process, between=None):
    a, b, B = at.a, at.b, at.breadth

    def right(slot):
        return remote(panel.at[slot], panel.at[slot], send.at[0, slot], recv.at[slot], at.r, at.c + B)

    def left(slot):
        return remote(panel.at[slot], panel.at[slot], send.at[1, slot], recv.at[slot], at.r, at.c - B)

    def over(slot, k):
        return remote(panel.at[slot], panel.at[slot], send.at[1 + k, slot], recv.at[slot], at.r, a * B + at.beside(k))

    def arrived(slot):
        remote(panel.at[slot], panel.at[slot], send.at[0, slot], recv.at[slot], at.r, at.c).wait_recv()

    @pl.when(a < LINE - 1)
    def _():
        right(at.c).start()

    @pl.when(a > 0)
    def _():
        left(at.c).start()

    for k in range(1, B):
        over(at.c, k).start()
    process(at.c)

    def beside(s):
        for sign in (-1, 1) if s else (1,):
            far = a + sign * s

            @pl.when((far >= 0) & (far < LINE))
            def _():
                for k in range(1, B):
                    slot = far * B + at.beside(k)
                    arrived(slot)
                    process(slot)

    for s in range(1, LINE):

        @pl.when(a - s >= 0)
        def _():
            slot = (a - s) * B + b
            arrived(slot)

            @pl.when(a < LINE - 1)
            def _():
                right(slot).start()

            for k in range(1, B):
                over(slot, k).start()

        @pl.when(a + s < LINE)
        def _():
            slot = (a + s) * B + b
            arrived(slot)

            @pl.when(a > 0)
            def _():
                left(slot).start()

            for k in range(1, B):
                over(slot, k).start()

        if between is not None and s == 1:
            between()
        for sign in (-1, 1):
            far = a + sign * s

            @pl.when((far >= 0) & (far < LINE))
            def _():
                process(far * B + b)

        beside(s - 1)
    beside(LINE - 1)

    def drain():
        for s in range(LINE):

            @pl.when((a - s >= 0) & (a < LINE - 1))
            def _():
                right((a - s) * B + b).wait_send()

            @pl.when((a + s < LINE) & (a > 0))
            def _():
                left((a + s) * B + b).wait_send()

        for s in range(LINE):
            for k in range(1, B):
                over(s * B + b, k).wait_send()

    return drain


class Across:
    def __init__(self, at, panel, send, recv):
        self.at, self.panel, self.send, self.recv = at, panel, send, recv
        self.chips = at.rows // 2
        self.core, self.chip = at.r % 2, at.r // 2
        self.sibling = self.chip * 2 + 1 - self.core

    def far(self, k):
        return ((self.chip + k) % self.chips) * 2 + self.core

    def far_pair(self, k):
        return ((self.chip + k) % self.chips) * 2 + 1 - self.core

    def go(self, slot, lane, row):
        ref = self.panel.at[slot]
        return remote(ref, ref, self.send.at[lane, slot], self.recv.at[slot], row, self.at.c)

    def arrived(self, slot):
        self.go(slot, 0, self.at.r).wait_recv()

    def start(self):
        for k in range(1, self.chips):
            self.go(self.at.r, k, self.far(k)).start()
        self.go(self.at.r, 0, self.sibling).start()

    def forward(self, process=None):
        for k in range(1, self.chips):
            slot = self.far(self.chips - k)
            self.arrived(slot)
            self.go(slot, 0, self.sibling).start()
            if process is not None:
                process(slot)

    def finish(self, process=None):
        self.arrived(self.sibling)
        if process is not None:
            process(self.sibling)
        for k in range(1, self.chips):
            slot = self.far_pair(k)
            self.arrived(slot)
            if process is not None:
                process(slot)

    def drain(self):
        for k in range(1, self.chips):
            self.go(self.at.r, k, self.far(k)).wait_send()
            self.go(self.far(k), 0, self.sibling).wait_send()
        self.go(self.at.r, 0, self.sibling).wait_send()


def first_kernel(
    rows, cols, left, grad, right, lpanel, rpanel, out, stage, partial, lsend, lrecv, rsend, rrecv, psend, precv
):
    at = Place(rows, cols)
    q = cols // rows
    n = left.shape[1]
    tile = tile_of(n, 128)
    at.greet(True, True)
    lpanel[at.c] = left[...]
    rpanel[at.r] = right[...]
    across = Across(at, rpanel, rsend, rrecv)
    across.start()

    def send(slot):
        to, t = slot // q, slot % q
        return remote(stage.at[slot], partial.at[at.r, t], psend.at[slot], precv.at[at.r, t], to, at.c)

    def process(slot):
        def step(i, _):
            span = pl.ds(pl.multiple_of(i * tile, tile), tile)
            stage[slot, span, :] = lax.dot_general(
                lpanel[slot, :, span], grad[...], (((0,), (0,)), ((), ())), preferred_element_type=F32
            ).astype(BF16)
            return 0

        lax.fori_loop(0, n // tile, step, 0)

        @pl.when(slot // q != at.r)
        def _():
            send(slot).start()

    drain = gather_along(at, lpanel, lsend, lrecv, process, across.forward)
    across.finish()
    for k in range(1, rows):
        for t in range(q):
            src = at.row_peer(k)
            ref = partial.at[src, t]
            remote(ref, ref, psend.at[0], precv.at[src, t], at.r, at.c).wait_recv()
    part = tile_of(n, 64)
    for t in range(q):

        def add(i, _):
            span = pl.ds(pl.multiple_of(i * part, part), part)
            total = stage[at.r * q + t, span, :].astype(F32)
            for k in range(1, rows):
                total += partial[at.row_peer(k), t, span, :].astype(F32)
            out[pl.ds(pl.multiple_of(t * n + i * part, part), part), :] = total.astype(BF16)
            return 0

        lax.fori_loop(0, n // part, add, 0)
    for k in range(1, rows):
        for t in range(q):
            send(at.row_peer(k) * q + t).wait_send()
    drain()
    across.drain()


def second_kernel(rows, cols, lr, rpanel, out, panel, send, recv):
    at = Place(rows, cols)
    q = cols // rows
    m, n = lr.shape
    tile = tile_of(m, 256) if m % 256 == 0 else tile_of(m, 128)
    at.greet(False, True)
    panel[at.c] = lr[...]
    out[...] = jnp.zeros_like(out)

    def process(slot):
        to, t = slot // q, slot % q
        depth = pl.ds(pl.multiple_of(t * n, n), n)

        def step(i, _):
            span = pl.ds(pl.multiple_of(i * tile, tile), tile)
            out[span, :] += jnp.dot(panel[slot, span, :], rpanel[to, depth, :], preferred_element_type=F32)
            return 0

        lax.fori_loop(0, m // tile, step, 0)

    gather_along(at, panel, send, recv, process)()


def third_kernel(
    rows, cols, parts, d, lpanel, rpanel, out, dpanel, total, back, near, line, dsend, drecv, nsend, nrecv, zsend, zrecv
):
    at = Place(rows, cols)
    a, B = at.a, at.breadth
    q = cols // rows
    m, n = d.shape
    tile = tile_of(m, 256) if m % 256 == 0 else tile_of(m, 128)
    high = m // parts
    fine = tile_of(high, 128)
    at.greet(True, True)
    dpanel[at.r] = d[...]
    across = Across(at, dpanel, dsend, drecv)
    across.start()
    total[...] = jnp.zeros_like(total)

    def gain(slot):
        def step(i, _):
            span = pl.ds(pl.multiple_of(i * tile, tile), tile)
            value = total[span, :]
            for t in range(q):
                value += jnp.dot(
                    lpanel[slot * q + t, span, :], dpanel[slot, t * n : (t + 1) * n, :], preferred_element_type=F32
                )
            total[span, :] = value
            return 0

        lax.fori_loop(0, m // tile, step, 0)

    gain(at.r)
    across.forward(gain)
    across.finish(gain)
    back[...] = total[...].astype(BF16)

    def over(k, target, h):
        rows_of = pl.ds(h * high, high)
        return remote(
            near.at[k - 1, 0, target, rows_of],
            near.at[k - 1, 1, target, rows_of],
            nsend.at[k - 1, target, h],
            nrecv.at[k - 1, target, h],
            at.r,
            a * B + at.beside(k),
        )

    def term(i, col):
        to, t = col // q, col % q
        return lax.dot_general(
            back[pl.ds(pl.multiple_of(i, fine), fine), :],
            rpanel[to, pl.ds(pl.multiple_of(t * n, n), n), :],
            (((1,), (1,)), ((), ())),
            preferred_element_type=F32,
        )

    order = []
    low, top = 0, LINE - 1
    while low <= top:
        order += [top, low] if low < top else [low]
        low, top = low + 1, top - 1
    pieces = [(target, h) for target in order for h in range(parts)]
    for target, h in pieces:
        for k in range(1, B):

            def fill(i, _):
                at_row = h * high + i * fine
                near[k - 1, 0, target, pl.ds(pl.multiple_of(at_row, fine), fine), :] = term(
                    at_row, target * B + at.beside(k)
                ).astype(BF16)
                return 0

            lax.fori_loop(0, high // fine, fill, 0)
            over(k, target, h).start()

    def shift(target, h, step):
        rows_of = pl.ds(h * high, high)
        slot = target if step > 0 else jnp.where(a - 1 == target, LINE, target)
        return remote(
            near.at[0, 1, target, rows_of],
            line.at[slot, rows_of],
            zsend.at[target, h],
            zrecv.at[slot, h],
            at.r,
            at.c + step * B,
        )

    def landed(slot, h):
        ref = line.at[slot, pl.ds(h * high, high)]
        remote(ref, ref, zsend.at[0, h], zrecv.at[slot, h], at.r, at.c).wait_recv()

    for target, h in pieces:
        for k in range(1, B):
            over(k, target, h).wait_recv()

        def combine(extra):
            def add(i, _):
                at_row = h * high + i * fine
                span = pl.ds(pl.multiple_of(at_row, fine), fine)
                value = term(at_row, target * B + at.b)
                for k in range(1, B):
                    value += near[k - 1, 1, target, span, :].astype(F32)
                if extra:
                    value += line[target, span, :].astype(F32)
                near[0, 1, target, span, :] = value.astype(BF16)
                return 0

            lax.fori_loop(0, high // fine, add, 0)

        def alone():
            combine(False)

        def joined():
            landed(target, h)
            combine(True)

        if target > 0:

            @pl.when(a == 0)
            def _():
                alone()
                shift(target, h, 1).start()

            @pl.when((a > 0) & (a < target))
            def _():
                joined()
                shift(target, h, 1).start()

        if target < LINE - 1:

            @pl.when(a == LINE - 1)
            def _():
                alone()
                shift(target, h, -1).start()

            @pl.when((a < LINE - 1) & (a > target))
            def _():
                joined()
                shift(target, h, -1).start()

        @pl.when(a == target)
        def _():
            alone()

    for h in range(parts):

        @pl.when(a > 0)
        def _():
            landed(a, h)

        @pl.when(a < LINE - 1)
        def _():
            landed(LINE, h)

        def last(use_left, use_right):
            def add(i, _):
                span = pl.ds(pl.multiple_of(h * high + i * fine, fine), fine)
                value = near[0, 1, a, span, :].astype(F32)
                if use_left:
                    value += line[a, span, :].astype(F32)
                if use_right:
                    value += line[LINE, span, :].astype(F32)
                out[span, :] = value.astype(BF16)
                return 0

            lax.fori_loop(0, high // fine, add, 0)

        pl.when(a == 0)(functools.partial(last, False, True))
        pl.when(a == LINE - 1)(functools.partial(last, True, False))
        pl.when((a > 0) & (a < LINE - 1))(functools.partial(last, True, True))

    for target, h in pieces:
        for k in range(1, B):
            over(k, target, h).wait_send()

        @pl.when(a != target)
        def _():
            shift(target, h, 1).wait_send()

    across.drain()


def call(kernel, number, outs, ins, scratch, flops):
    vmem = pl.BlockSpec(memory_space=pltpu.VMEM)
    return pl.pallas_call(
        kernel,
        out_shape=outs,
        in_specs=[vmem] * ins,
        out_specs=jax.tree.map(lambda _: vmem, outs),
        scratch_shapes=scratch,
        compiler_params=pltpu.CompilerParams(
            collective_id=number, has_side_effects=True, vmem_limit_bytes=60 * 1024 * 1024
        ),
        cost_estimate=pl.CostEstimate(flops=flops, bytes_accessed=30_000_000, transcendentals=0),
    )


def body(rows, cols, gradient, left_basis, right_basis, first_moment, second_moment):
    m, n = gradient.shape
    q = cols // rows
    B = cols // LINE
    dma = pltpu.SemaphoreType.DMA
    shape = jax.ShapeDtypeStruct
    flops = 2 * m * n * m * rows
    chips = rows // 2
    lpanel, rpanel, left_rotated = call(
        functools.partial(first_kernel, rows, cols),
        0,
        (shape((cols, m, n), BF16), shape((rows, m, n), BF16), shape((m, n), BF16)),
        3,
        [
            pltpu.VMEM((cols, n, n), BF16),
            pltpu.VMEM((rows, q, n, n), BF16),
            dma((1 + B, cols)),
            dma((cols,)),
            dma((chips, rows)),
            dma((rows,)),
            dma((cols,)),
            dma((rows, q)),
        ],
        flops,
    )(left_basis, gradient, right_basis)
    rotated = call(
        functools.partial(second_kernel, rows, cols),
        1,
        shape((m, n), F32),
        2,
        [pltpu.VMEM((cols, m, n), BF16), dma((1 + B, cols)), dma((cols,))],
        flops,
    )(left_rotated, rpanel)
    new_first = 0.9 * first_moment + 0.1 * rotated
    new_second = 0.95 * second_moment + 0.05 * rotated * rotated
    first_fix = 1.0 - 0.9**STEP
    second_fix = 1.0 - 0.95**STEP
    direction = (new_first / first_fix / (jnp.sqrt(new_second / second_fix) + 1e-08)).astype(BF16)
    parts = 2
    update = call(
        functools.partial(third_kernel, rows, cols, parts),
        2,
        shape((m, n), BF16),
        3,
        [
            pltpu.VMEM((rows, m, n), BF16),
            pltpu.VMEM((m, n), F32),
            pltpu.VMEM((m, n), BF16),
            pltpu.VMEM((B - 1, 2, LINE, m, n), BF16),
            pltpu.VMEM((LINE + 1, m, n), BF16),
            dma((chips, rows)),
            dma((rows,)),
            dma((B - 1, LINE, parts)),
            dma((B - 1, LINE, parts)),
            dma((LINE, parts)),
            dma((LINE + 1, parts)),
        ],
        2 * flops,
    )(direction, lpanel, rpanel)
    return (update, new_first, new_second)


def solution(mesh):
    spec = P("row", "col")
    return jax.shard_map(
        functools.partial(body, mesh.shape["row"], mesh.shape["col"]),
        mesh=mesh,
        in_specs=(spec,) * 5,
        out_specs=(spec,) * 3,
        check_vma=False,
    )
```

time: 1090 us -> 582 us (0.53)
  waiting for transfers between devices: 983 us -> 0 us
  Pallas kernels: 0 us -> 571 us
  matrix products: 80.4 us -> 0 us
  between operations: 14.1 us -> 0.67 us
    pallas_call x0 -> x3, Pallas kernels: none -> 571 us  [the longest x1 244 us: body(): call(functools.partial(third_kernel, rows, cols, parts), 2, shape((m, n),...]
    reduce_scatter x2 -> x0, waiting for transfers between devices: 519 us -> none  [the longest x1 417 us: body(): lax.psum_scatter(partial_terms, 'col', scatter_dimension=1, tiled=True)]
    all_gather x4 -> x0, waiting for transfers between devices: 462 us -> none  [the longest x1 184 us: body(): left_panel = lax.all_gather(left_basis, 'col', axis=1, tiled=True)]
    dot_general x3 -> x0, matrix products: 80.4 us -> none  [the longest x1 44 us: body(): lax.dot_general(back_left, right_panel, (((1,), (1,)), ((), ())), preferr...]
  transfers between devices with their start and end apart: 6 -> 0, of which waited for: 6 -> 0; matrix products, arithmetic and copies ran while one was open for 0% -> 0% of each run, Pallas kernels for 0% -> 0%
where the time goes in v2:
time: 582 us
  Pallas kernels  571 us (98%)
  other arithmetic  7.59 us (1%)
    pallas_call x1, Pallas kernels, body(): call(functools.partial(third_kernel, rows, cols, parts), 2, shape((m, n),...  244 us
    pallas_call x1, Pallas kernels, body(): call(functools.partial(first_kernel, rows, cols), 0, (shape((cols, m, n),...  175 us
    pallas_call x1, Pallas kernels, body(): call(functools.partial(second_kernel, rows, cols), 1, shape((m, n), F32),...  152 us

profile of v2, /device:TPU:8, one launch (start us, length us, event | category | flops | bytes accessed | tf_op | source)
XLA Modules:
  0.0 581.9 jit_solution(12780747209699682384)
XLA Ops:
  0.6 175.0 %shard_map.76 = (bf16[8,1280,640]{2,1,0:T(8,128)(2,1)}, bf16[4,1280,640]{2,1,0:T(8,128)(2,1)}, bf16[1280,640]{1,0:T(8,128)(2,1)}) custom-call(bf16[1280,640]{1,0:T(8,128)(2,1)} %left.1, bf16[1280,640]{1,0:T(8,128)(2,1)} %grad.1, bf16[1280,640]{1,0:T(8,128)(2,1)} %right.1), custom_call_target="tpu_custom_call" | custom-call | flops 8388608000 | bytes 30000000 | tf_op jit(solution)/shard_map/pallas_call | solution.py:509
  175.7 0.0 copy-start
  175.7 151.7 %shard_map.77 = f32[1280,640]{1,0:T(8,128)} custom-call(bf16[1280,640]{1,0:T(8,128)(2,1)} %get-tuple-element.6.lr, bf16[4,1280,640]{2,1,0:T(8,128)(2,1)} %get-tuple-element.7.rpanel), custom_call_target="tpu_custom_call" | custom-call | flops 8388608000 | bytes 30000000 | tf_op jit(solution)/shard_map/pallas_call | solution.py:526
  327.4 0.0 copy-done
  327.4 7.6 %divide_convert_fusion = (bf16[1280,640]{1,0:T(8,128)(2,1)}, f32[1280,640]{1,0:T(8,128)}, f32[1280,640]{1,0:T(8,128)}) fusion(f32[1280,640]{1,0:T(8,128)} %shard_map.77, f32[1280,640]{1,0:T(8,128)S(1)} %copy-done, f32[1280,640]{1,0:T(8,128)} %param.9), kind=kLoop, calls=%fused_computation.2 | loop fusion | flops 9830400 | bytes 18022400 | tf_op jit(solution)/shard_map/convert_element_type | solution.py:538
  335.0 244.1 %shard_map.78 = bf16[1280,640]{1,0:T(8,128)(2,1)} custom-call(bf16[1280,640]{1,0:T(8,128)(2,1)} %get-tuple-element.9.d, bf16[8,1280,640]{2,1,0:T(8,128)(2,1)} %get-tuple-element.8.lpanel, bf16[4,1280,640]{2,1,0:T(8,128)(2,1)} %get-tuple-element.7.rpanel), custom_call_target="tpu_custom_call" | custom-call | flops 16777216000 | bytes 30000000 | tf_op jit(solution)/shard_map/pallas_call | solution.py:540
  579.1 2.7 copy.9
Async XLA Ops:
  175.7 151.8 %copy-start = (f32[1280,640]{1,0:T(8,128)S(1)}, f32[1280,640]{1,0:T(8,128)}, u32[]{:S(2)}) copy-start(f32[1280,640]{1,0:T(8,128)} %param.8) | copy-start | bytes 9830404

commit v3 on v2

--- a/solution.py
+++ b/solution.py
@@ -94,6 +94,39 @@
     def arrived(slot):
         remote(panel.at[slot], panel.at[slot], send.at[0, slot], recv.at[slot], at.r, at.c).wait_recv()
 
+    half = panel.shape[1] // 2
+    mate = a + 1 - 2 * (a % 2)
+
+    def over_half(slot, k):
+        ref = panel.at[slot, pl.ds(0, half)]
+        return remote(ref, ref, send.at[1 + k, slot], recv.at[slot], at.r, a * B + at.beside(k))
+
+    def to_mate(slot):
+        ref = panel.at[slot, pl.ds(half, half)]
+        return remote(ref, ref, send.at[0, slot], recv.at[LINE * B + slot], at.r, mate * B + b)
+
+    def arrived_halves(slot):
+        for h in range(2):
+            ref = panel.at[slot, pl.ds(h * half, half)]
+            remote(ref, ref, send.at[0, slot], recv.at[h * LINE * B + slot], at.r, at.c).wait_recv()
+
+    def sides(far, start):
+        for k in range(1, B):
+
+            @pl.when(far == mate)
+            def _():
+                start(over_half(far * B + b, k))
+
+            @pl.when(far != mate)
+            def _():
+                start(over(far * B + b, k))
+
+    def begin(copy):
+        copy.start()
+
+    def leave(copy):
+        copy.wait_send()
+
     @pl.when(a < LINE - 1)
     def _():
         right(at.c).start()
@@ -114,7 +147,13 @@
             def _():
                 for k in range(1, B):
                     slot = far * B + at.beside(k)
-                    arrived(slot)
+                    if s == 1:
+                        pl.when(far == mate)(functools.partial(arrived_halves, slot))
+                        pl.when(far != mate)(functools.partial(arrived, slot))
+                    else:
+                        arrived(slot)
+                    if s == 0:
+                        to_mate(slot).start()
                     process(slot)
 
     for s in range(1, LINE):
@@ -128,8 +167,7 @@
             def _():
                 right(slot).start()
 
-            for k in range(1, B):
-                over(slot, k).start()
+            sides(a - s, begin)
 
         @pl.when(a + s < LINE)
         def _():
@@ -140,10 +178,9 @@
             def _():
                 left(slot).start()
 
-            for k in range(1, B):
-                over(slot, k).start()
-
-        if between is not None and s == 1:
+            sides(a + s, begin)
+
+        if between is not None and s == LINE - 2:
             between()
         for sign in (-1, 1):
             far = a + sign * s
@@ -167,8 +204,9 @@
                 left((a + s) * B + b).wait_send()
 
         for s in range(LINE):
-            for k in range(1, B):
-                over(s * B + b, k).wait_send()
+            sides(s, leave)
+        for k in range(1, B):
+            to_mate(a * B + at.beside(k)).wait_send()
 
     return drain
 
@@ -515,7 +553,7 @@
             pltpu.VMEM((cols, n, n), BF16),
             pltpu.VMEM((rows, q, n, n), BF16),
             dma((1 + B, cols)),
-            dma((cols,)),
+            dma((2 * cols,)),
             dma((chips, rows)),
             dma((rows,)),
             dma((cols,)),
@@ -528,7 +566,7 @@
         1,
         shape((m, n), F32),
         2,
-        [pltpu.VMEM((cols, m, n), BF16), dma((1 + B, cols)), dma((cols,))],
+        [pltpu.VMEM((cols, m, n), BF16), dma((1 + B, cols)), dma((2 * cols,))],
         flops,
     )(left_rotated, rpanel)
     new_first = 0.9 * first_moment + 0.1 * rotated

time: 582 us -> 610 us (1.048)
  Pallas kernels: 571 us -> 599 us
    pallas_call x1, Pallas kernels: 244 us -> 273 us  [body(): call(functools.partial(third_kernel, rows, cols, parts), 2, shape((m, n),...]
    pallas_call x1, Pallas kernels: 175 us -> 158 us  [body(): call(functools.partial(first_kernel, rows, cols), 0, (shape((cols, m, n),...]
    pallas_call x1, Pallas kernels: 152 us -> 168 us  [body(): call(functools.partial(second_kernel, rows, cols), 1, shape((m, n), F32),...]
where the time goes in v3:
time: 610 us
  Pallas kernels  599 us (98%)
  other arithmetic  7.59 us (1%)
    pallas_call x1, Pallas kernels, body(): call(functools.partial(third_kernel, rows, cols, parts), 2, shape((m, n),...  273 us
    pallas_call x1, Pallas kernels, body(): call(functools.partial(second_kernel, rows, cols), 1, shape((m, n), F32),...  168 us
    pallas_call x1, Pallas kernels, body(): call(functools.partial(first_kernel, rows, cols), 0, (shape((cols, m, n),...  158 us

profile of v3, /device:TPU:8, one launch (start us, length us, event | category | flops | bytes accessed | tf_op | source)
XLA Modules:
  0.0 609.7 jit_solution(7294309643102398866)
XLA Ops:
  0.6 157.5 %shard_map.76 = (bf16[8,1280,640]{2,1,0:T(8,128)(2,1)}, bf16[4,1280,640]{2,1,0:T(8,128)(2,1)}, bf16[1280,640]{1,0:T(8,128)(2,1)}) custom-call(bf16[1280,640]{1,0:T(8,128)(2,1)} %left.1, bf16[1280,640]{1,0:T(8,128)(2,1)} %grad.1, bf16[1280,640]{1,0:T(8,128)(2,1)} %right.1), custom_call_target="tpu_custom_call" | custom-call | flops 8388608000 | bytes 30000000 | tf_op jit(solution)/shard_map/pallas_call | solution.py:547
  158.2 0.0 copy-start
  158.2 168.2 %shard_map.77 = f32[1280,640]{1,0:T(8,128)} custom-call(bf16[1280,640]{1,0:T(8,128)(2,1)} %get-tuple-element.6.lr, bf16[4,1280,640]{2,1,0:T(8,128)(2,1)} %get-tuple-element.7.rpanel), custom_call_target="tpu_custom_call" | custom-call | flops 8388608000 | bytes 30000000 | tf_op jit(solution)/shard_map/pallas_call | solution.py:564
  326.4 0.0 copy-done
  326.4 7.6 %divide_convert_fusion = (bf16[1280,640]{1,0:T(8,128)(2,1)}, f32[1280,640]{1,0:T(8,128)}, f32[1280,640]{1,0:T(8,128)}) fusion(f32[1280,640]{1,0:T(8,128)} %shard_map.77, f32[1280,640]{1,0:T(8,128)S(1)} %copy-done, f32[1280,640]{1,0:T(8,128)} %param.9), kind=kLoop, calls=%fused_computation.2 | loop fusion | flops 9830400 | bytes 18022400 | tf_op jit(solution)/shard_map/convert_element_type | solution.py:576
  334.0 272.9 %shard_map.78 = bf16[1280,640]{1,0:T(8,128)(2,1)} custom-call(bf16[1280,640]{1,0:T(8,128)(2,1)} %get-tuple-element.9.d, bf16[8,1280,640]{2,1,0:T(8,128)(2,1)} %get-tuple-element.8.lpanel, bf16[4,1280,640]{2,1,0:T(8,128)(2,1)} %get-tuple-element.7.rpanel), custom_call_target="tpu_custom_call" | custom-call | flops 16777216000 | bytes 30000000 | tf_op jit(solution)/shard_map/pallas_call | solution.py:578
  607.0 2.7 copy.9
Async XLA Ops:
  158.2 168.2 %copy-start = (f32[1280,640]{1,0:T(8,128)S(1)}, f32[1280,640]{1,0:T(8,128)}, u32[]{:S(2)}) copy-start(f32[1280,640]{1,0:T(8,128)} %param.8) | copy-start | bytes 9830404
